TPU v7x, 32 devices: a whole 2x2x4 slice. The times are simulated.
32 devices in a mesh: dp: 8 (over y, x, core), mp: 4 (over z).
Axes of the slice: x: 2, y: 2, z: 4, core: 2. Of those that a mesh axis runs over, the one named last changes fastest.
Arguments:
- response_query: bfloat16 [384, 8, 6144], P('dp', None, 'mp'), may hold values from -80 to 80, as said below
- response_keys: bfloat16 [2, 384, 8, 768], P(None, 'dp'), may hold values from -8 to 8
- prompt_cache: bfloat16 [2, 8, 1024, 768], P(None, 'dp'), may hold values from -6 to 6
- lengths: int32 [384], P('dp'), may hold values from 1 to 8, as said below
- owners: int32 [384], P('dp'), may hold values from 0 to 7, as said below
- pairing: int32 [384], replicated, may hold values from 0 to 383, each once
- residual: bfloat16 [384, 8192], P(None, 'dp'), may hold values from -90 to 90
- output_weight: bfloat16 [6144, 8192], P('mp', 'dp'), may hold values from -0.3125 to 0.3125
- norm_gain: float32 [8192], P('dp'), may hold values from 0.1 to 1.9
- reward_head: float32 [8192], P('dp'), may hold values from -0.0625 to 0.0625
Outputs:
- attention_rows: bfloat16 [384, 8, 6144], P('dp', None, 'mp')
- rewards: float32 [384], replicated
- pair_loss: float32 [], replicated
- weight_gradient: float32 [6144, 8192], P('mp', 'dp')
- head_gradient: float32 [8192], P('dp')
- pooled_gradient: float32 [384, 6144], P('dp', 'mp')
Inputs may be any that keep to these rules, and one draw needn't show every extreme that they name: `response_query`: drawn jointly with response_keys. `lengths`: every dp index holds a response of length 8. The responses of one dp index spread over owners as evenly as possible: each owner receives at most 6 of them, and some owner receives exactly 6.
All inputs are finite; a program needn't handle non-finite values.
Results may differ from a plain program's by a relative error of at most 0.0056.
Values may be sent and summed in bfloat16 or wider, within the bound.
A program may use at most 64 MiB of HBM per device.

v0:
```python
import math
import jax
import jax.numpy as jnp
from jax import lax
from jax.sharding import PartitionSpec as P

D = 8192
HD = 128
Q_HEADS = 48
KV_HEADS = 6
EPSILON = 1e-05


def bradley_terry(rewards, pairing):
    chosen = pairing[0::2]
    rejected = pairing[1::2]
    margin = rewards[chosen] - rewards[rejected]
    loss_value = jnp.mean(jax.nn.softplus(-margin))
    slope = -jax.nn.sigmoid(-margin) / margin.shape[0]
    reward_slope = jnp.zeros_like(rewards).at[chosen].add(slope).at[rejected].add(-slope)
    return (loss_value, reward_slope)


def shards(
    response_query,
    response_keys,
    prompt_cache,
    lengths,
    owners,
    pairing,
    residual,
    output_weight,
    norm_gain,
    reward_head,
):
    groups = lax.axis_size("dp")
    model_rank = lax.axis_index("mp")
    held_count = response_query.shape[0]
    slot_count = response_query.shape[1]
    head_width = response_query.shape[2]
    local_heads = head_width // HD
    group_size = Q_HEADS // KV_HEADS
    per_owner = (held_count + groups - 1) // groups
    if group_size % local_heads == 0:
        window = 1
    elif local_heads % group_size == 0:
        window = local_heads // group_size
    else:
        window = min(KV_HEADS, (local_heads - 1) // group_size + 2)
    first_head = jnp.minimum(model_rank * local_heads // group_size, KV_HEADS - window)
    head_slot = (model_rank * local_heads + jnp.arange(local_heads)) // group_size - first_head
    score_scale = 1.0 / math.sqrt(HD)
    own_window = lax.dynamic_slice_in_dim(response_keys, first_head * HD, window * HD, 3)
    spread = own_window.reshape(2, held_count, slot_count, window, HD)
    picked = jnp.take(spread, head_slot, axis=3).reshape(
        2, held_count, slot_count, local_heads * HD
    )
    key_pick = jnp.arange(local_heads)
    outgoing_keys = jnp.concatenate([picked[0], picked[1]], axis=-1)
    positions = jnp.arange(held_count)
    earlier = (owners[None, :] == owners[:, None]) & (positions[None, :] < positions[:, None])
    target = owners * per_owner + jnp.sum(earlier, axis=1)
    capacity = groups * per_owner
    query_buffer = (
        jnp.zeros((capacity, slot_count, head_width), jnp.bfloat16).at[target].set(response_query)
    )
    query_buffer = query_buffer.reshape(groups, per_owner, slot_count, head_width)
    key_buffer = (
        jnp.zeros((capacity, slot_count, 2 * local_heads * HD), jnp.bfloat16)
        .at[target]
        .set(outgoing_keys)
    )
    key_buffer = key_buffer.reshape(groups, per_owner, slot_count, 2 * local_heads * HD)
    length_buffer = (
        jnp.zeros((capacity,), jnp.int32).at[target].set(lengths).reshape(groups, per_owner)
    )
    prefix = lax.dynamic_slice_in_dim(prompt_cache[:, 0], first_head * HD, window * HD, 2)
    query_in = lax.all_to_all(query_buffer, "dp", split_axis=0, concat_axis=0, tiled=True)
    keys_in = lax.all_to_all(key_buffer, "dp", split_axis=0, concat_axis=0, tiled=True)
    length_in = lax.all_to_all(length_buffer, "dp", split_axis=0, concat_axis=0, tiled=True)
    sources = query_in.shape[0]
    item_count = query_in.shape[1]
    blocks = sources * item_count
    row_count = blocks * slot_count
    queries = query_in.reshape(blocks, slot_count, local_heads, HD)
    own_keys = keys_in.reshape(blocks, slot_count, 2, local_heads, HD)
    live_length = length_in.reshape(blocks)
    offsets = jnp.arange(slot_count)
    allowed = (offsets[None, None, :] <= offsets[None, :, None]) & (
        offsets[None, None, :] < live_length[:, None, None]
    )
    valid_rows = offsets[None, :] < live_length[:, None]

    def one_head(head_index):
        query_head = lax.dynamic_index_in_dim(queries, head_index, 2, keepdims=False)
        self_pair = lax.dynamic_index_in_dim(own_keys, key_pick[head_index], 3, keepdims=False)
        cache_pair = lax.dynamic_slice_in_dim(prefix, head_slot[head_index] * HD, HD, 2)
        flat_query = query_head.reshape(row_count, HD)
        far_scores = (
            lax.dot_general(
                flat_query,
                cache_pair[0],
                (((1,), (1,)), ((), ())),
                preferred_element_type=jnp.float32,
            )
            * score_scale
        )
        near_scores = (
            jnp.einsum(
                "bth,bsh->bts", query_head, self_pair[:, :, 0], preferred_element_type=jnp.float32
            )
            * score_scale
        )
        near_scores = jnp.where(allowed, near_scores, -jnp.inf)
        row_top = jnp.maximum(
            jnp.max(far_scores, axis=1).reshape(blocks, slot_count), jnp.max(near_scores, axis=2)
        )
        far_weight = jnp.exp(far_scores - row_top.reshape(row_count, 1))
        near_weight = jnp.exp(near_scores - row_top[:, :, None])
        weight_total = jnp.sum(far_weight, axis=1).reshape(blocks, slot_count) + jnp.sum(
            near_weight, axis=2
        )
        output = jnp.dot(
            far_weight.astype(jnp.bfloat16), cache_pair[1], preferred_element_type=jnp.float32
        ).reshape(blocks, slot_count, HD)
        output = output + jnp.einsum(
            "bts,bsh->bth",
            near_weight.astype(jnp.bfloat16),
            self_pair[:, :, 1],
            preferred_element_type=jnp.float32,
        )
        output = output / weight_total[:, :, None]
        return jnp.where(valid_rows[:, :, None], output, 0.0).astype(jnp.bfloat16)

    heads_out = lax.map(one_head, jnp.arange(local_heads))
    result = jnp.transpose(heads_out, (1, 2, 0, 3)).reshape(
        sources, item_count, slot_count, head_width
    )
    returned = lax.all_to_all(result, "dp", split_axis=0, concat_axis=0, tiled=True)
    attention_rows = returned.reshape(capacity, slot_count, head_width)[target]
    pooled_local = attention_rows[positions, lengths - 1]
    pooled_all = lax.all_gather(pooled_local, "dp", axis=0, tiled=True)
    partial_mix = jnp.dot(pooled_all, output_weight, preferred_element_type=jnp.float32)
    scaled_head = norm_gain * reward_head
    combined = lax.psum(partial_mix, "mp") + residual.astype(jnp.float32)
    square_sum = jnp.sum(combined * combined, axis=1)
    signal = jnp.sum(combined * scaled_head[None, :], axis=1)
    square_sum, signal = lax.psum((square_sum, signal), "dp")
    inverse = lax.rsqrt(square_sum / D + EPSILON)
    rewards = inverse * signal
    pair_loss, reward_slope = bradley_terry(rewards, pairing)
    direct_term = reward_slope * inverse
    norm_term = reward_slope * inverse * inverse * inverse * signal / D
    upstream = direct_term[:, None] * scaled_head[None, :] - norm_term[:, None] * combined
    head_gradient = jnp.sum(direct_term[:, None] * combined * norm_gain[None, :], axis=0)
    upstream_half = upstream.astype(jnp.bfloat16)
    weight_gradient = lax.dot_general(
        pooled_all, upstream_half, (((0,), (0,)), ((), ())), preferred_element_type=jnp.float32
    )
    pooled_gradient = lax.psum_scatter(
        lax.dot_general(
            upstream_half,
            output_weight,
            (((1,), (1,)), ((), ())),
            preferred_element_type=jnp.float32,
        ),
        "dp",
        scatter_dimension=0,
        tiled=True,
    )
    return (attention_rows, rewards, pair_loss, weight_gradient, head_gradient, pooled_gradient)


def solution(mesh):
    placed = (
        P("dp", None, "mp"),
        P(None, "dp", None, None),
        P(None, "dp", None, None),
        P("dp"),
        P("dp"),
        P(),
        P(None, "dp"),
        P("mp", "dp"),
        P("dp"),
        P("dp"),
    )
    return jax.shard_map(
        shards,
        mesh=mesh,
        in_specs=placed,
        out_specs=(P("dp", None, "mp"), P(), P(), P("mp", "dp"), P("dp"), P("dp", "mp")),
        check_vma=False,
    )
```

profile of v0, /device:TPU:0, one launch (start us, length us, event | category | flops | bytes accessed | tf_op | source)
XLA Modules:
  0.0 529.6 jit_solution(9194661605754231046)
XLA Ops:
  10.4 5.2 all-to-all-start
  18.1 3.6 gather_fusion
  21.8 3.4 select_bitcast_fusion
  26.2 7.2 %scatter_fusion = bf16[48,8,1536]{2,1,0:T(8,128)(2,1)} fusion(bf16[48,8,1536]{2,1,0:T(8,128)(2,1)} %broadcast_in_dim.88, s32[48]{0:T(128)S(1)} %compare_select_fusion.6, bf16[48,8,1536]{2,1,0:T(8,128)(2,1)} %param.12), kind=kCustom, calls=%fused_computation.6 | custom fusion | bytes 3539136 | tf_op jit(solution)/shard_map/scatter | solution.py:65
  33.4 4.2 all-to-all-start.1
  43.2 8.2 %scatter_fusion.1 = bf16[48,8,3072]{2,1,0:T(8,128)(2,1)} fusion(bf16[48,8,3072]{2,1,0:T(8,128)(2,1)} %broadcast_in_dim.89, s32[48]{0:T(128)S(1)} %compare_select_fusion.6, bf16[48,8,3072]{2,1,0:T(8,128)(2,1)} %pad_maximum_fusion), kind=kCustom, calls=%fused_computation.7 | custom fusion | bytes 7078080 | tf_op jit(solution)/shard_map/scatter | solution.py:71
  51.4 3.1 all-to-all-done.1
  54.5 4.4 all-to-all-start.2
  58.9 2.7 dynamic-slice_bitcast_fusion.4
  62.9 25.4 %all-to-all-done.2 = bf16[8,6,8,3072]{3,2,1,0:T(8,128)(2,1)} async-done(((bf16[8,6,8,3072]{3,2,1,0:T(8,128)(2,1)}), bf16[8,6,8,3072]{3,2,1,0:T(8,128)(2,1)}, u32[]{:S(2)}, u32[]{:S(2)}) %all-to-all-start.2) | async-done | bytes 2359328 | tf_op jit(solution)/shard_map/all_to_all | solution.py:79
  88.9 239.0 %while.13 = (s32[]{:T(128)}, bf16[12,48,8,128]{3,2,0,1:T(8,128)(2,1)}, s32[12]{0:T(128)}, bf16[48,8,12,128]{3,1,2,0:T(8,128)(2,1)}, s32[12]{0:T(128)}, /*index=5...) while((s32[]{:T(128)}, ...), condition=%wide.region_9.10_spmd.clone.clone, body=%wide.region_4.9_spmd.clone.clone.sunk | while | flops 205486080 | bytes 6827307 | solution.py:135
  94.0 2.5 fusion.67
  113.9 2.5 fusion.67
  133.8 2.5 fusion.67
  153.7 2.5 fusion.67
  173.7 2.5 fusion.67
  193.6 2.5 fusion.67
  213.5 2.5 fusion.67
  253.3 2.5 fusion.67
  293.2 2.5 fusion.67
  327.9 4.4 all-to-all-start.3
  332.4 16.7 %all-to-all-done.3 = bf16[8,6,8,1536]{3,2,1,0:T(8,128)(2,1)} async-done(((bf16[8,6,8,1536]{3,2,1,0:T(8,128)(2,1)}), bf16[8,6,8,1536]{3,2,1,0:T(8,128)(2,1)}, u32[]{:S(2)}, u32[]{:S(2)}) %all-to-all-start.3) | async-done | bytes 1179680 | tf_op jit(solution)/shard_map/all_to_all | solution.py:139
  349.2 3.0 gather_fusion.1
  352.1 3.2 gather_fusion.2
  355.4 23.6 %all-gather.2.cloned.1.call-done = bf16[384,1536]{1,0:T(8,128)(2,1)} async-done(((bf16[48,1536]{1,0:T(8,128)(2,1)}), bf16[384,1536]{1,0:T(8,128)(2,1)}) %all-gather.2.cloned.1.call-update) | async-done | bytes 1179664 | tf_op jit(solution)/shard_map/all_gather | solution.py:142
  378.9 3.8 fusion.44
  383.9 68.1 %all-reduce.3.cloned.1.call-done = f32[384,1024]{1,0:T(8,128)} async-done(((f32[384,1024]{1,0:T(8,128)}), f32[384,1024]{1,0:T(8,128)}) %all-reduce.3.cloned.1.call-update) | async-done | bytes 1572880 | tf_op jit(solution)/shard_map/psum | solution.py:145
  454.0 12.5 %all-reduce = (f32[384]{0:T(512)S(1)}, f32[384]{0:T(512)S(1)}) all-reduce(f32[384]{0:T(512)S(1)} %get-tuple-element.190, f32[384]{0:T(512)S(1)} %get-tuple-element.189), channel_id=1, replica_groups=mesh['dp'=8,'mp'=4] {'dp'}, use_global_device_ids=true, to_apply=%region_14.15 | all-reduce | flops 768 | bytes 6144 | tf_op jit(solution)/shard_map/psum | solution.py:148
  474.4 2.7 multiply_reduce_fusion
  477.9 2.9 fusion.46
  481.5 6.0 %fusion.45 = f32[1536,1024]{1,0:T(8,128)} fusion(bf16[384,1536]{1,0:T(8,128)(2,1)} %all-gather.2.cloned.1.call-done, bf16[384,1024]{1,0:T(8,128)(2,1)} %copy-done.3), kind=kOutput, calls=%fused_computation.102 | convolution fusion | flops 1207959552 | bytes 8257536 | tf_op jit(solution)/shard_map/dot_general | solution.py:157
  487.5 34.5 %reduce-scatter.2.cloned.1.call-done = f32[48,1536]{1,0:T(8,128)} async-done(((f32[384,1536]{1,0:T(8,128)}), f32[48,1536]{1,0:T(8,128)}) %reduce-scatter.2.cloned.1.call-update) | async-done | bytes 294928 | tf_op jit(solution)/shard_map/reduce_scatter | solution.py:160
  (365 shorter events, 187.0 us)
Async XLA Ops:
  7.2 371.8 %copy-start = (bf16[1536,1024]{1,0:T(8,128)(2,1)S(1)}, bf16[1536,1024]{1,0:T(8,128)(2,1)}, u32[]{:S(2)}) copy-start(bf16[1536,1024]{1,0:T(8,128)(2,1)} %param.19) | copy-start | bytes 9437188
  8.9 34.3 %copy-start.5 = (s32[48]{0:T(128)}, s32[48]{0:T(128)S(1)}, u32[]{:S(2)}) copy-start(s32[48]{0:T(128)S(1)} %compare_select_fusion.6) | copy-start | bytes 580
  10.4 23.0 %all-to-all-start = ((s32[8,1,6]{2,1,0:T(1,128)}), s32[8,1,6]{2,1,0:T(1,128)S(1)}, u32[]{:S(2)}, u32[]{:S(2)}) async-start(s32[8,1,6]{2,1,0:T(1,128)} %bitcast.10), calls=%async_computation | async-start | bytes 8192 | tf_op jit(solution)/shard_map/all_to_all | solution.py:80
  33.4 21.1 %all-to-all-start.1 = ((bf16[8,6,8,1536]{3,2,1,0:T(8,128)(2,1)}), bf16[8,6,8,1536]{3,2,1,0:T(8,128)(2,1)}, u32[]{:S(2)}, u32[]{:S(2)}) async-start(bf16[8,6,8,1536]{3,2,1,0:T(8,128)(2,1)} %bitcast.101), calls=%async_computation.1 | async-start | bytes 2359296 | tf_op jit(solution)/shard_map/all_to_all | solution.py:78
  54.5 33.8 %all-to-all-start.2 = ((bf16[8,6,8,3072]{3,2,1,0:T(8,128)(2,1)}), bf16[8,6,8,3072]{3,2,1,0:T(8,128)(2,1)}, u32[]{:S(2)}, u32[]{:S(2)}) async-start(bf16[8,6,8,3072]{3,2,1,0:T(8,128)(2,1)} %bitcast.100), calls=%async_computation.2 | async-start | bytes 4718592 | tf_op jit(solution)/shard_map/all_to_all | solution.py:79
  102.5 3.2 copy-start.2
  122.4 3.2 copy-start.2
  142.3 3.2 copy-start.2
  162.2 3.2 copy-start.2
  182.2 3.2 copy-start.2
  202.1 3.2 copy-start.2
  222.0 3.2 copy-start.2
  241.9 3.2 copy-start.2
  261.8 3.2 copy-start.2
  281.8 3.2 copy-start.2
  301.7 3.2 copy-start.2
  321.6 3.2 copy-start.2
  327.9 4.4 copy-start.6
  327.9 4.5 copy-start.9
  327.9 21.2 %all-to-all-start.3 = ((bf16[8,6,8,1536]{3,2,1,0:T(8,128)(2,1)}), bf16[8,6,8,1536]{3,2,1,0:T(8,128)(2,1)}, u32[]{:S(2)}, u32[]{:S(2)}) async-start(bf16[8,6,8,1536]{3,2,1,0:T(8,128)(2,1)} %bitcast.12), calls=%async_computation.3 | async-start | bytes 2359296 | tf_op jit(solution)/shard_map/all_to_all | solution.py:139
  332.3 46.6 %all-gather.2.cloned.1.call-start = ((), (), s32[]{:S(2)}) async-start(), calls=%async_computation.5 | async-start | bytes 1327104 | tf_op jit(solution)/shard_map/all_gather | solution.py:142
  355.3 96.7 %all-reduce.3.cloned.1.call-start = ((), (), s32[]{:S(2)}) async-start(), calls=%async_computation.6 | async-start | bytes 3145728 | tf_op jit(solution)/shard_map/psum | solution.py:145
  382.7 0.7 copy-start.8
  382.7 1.1 copy-start.4
  382.7 1.1 copy-start.7
  382.8 139.2 %reduce-scatter.2.cloned.1.call-start = ((), (), s32[]{:S(2)}) async-start(), calls=%async_computation.7 | async-start | bytes 2654208 | tf_op jit(solution)/shard_map/reduce_scatter | solution.py:160
  466.5 7.8 %copy-start.1 = (f32[384]{0:T(512)}, f32[384]{0:T(512)S(1)}, u32[]{:S(2)}) copy-start(f32[384]{0:T(512)S(1)} %fusion.33) | copy-start | bytes 4612
  477.0 0.9 copy-start.3
Sparse Core Ops, SparseCore 0:
  355.4 23.4 all-gather.1
  382.9 69.0 all-reduce.2
  480.9 40.9 reduce-scatter.1
where the time goes:
time: 534 us; the launch traced here: 530 us
  waiting for transfers between devices  171 us (32%)
  local copies, waits for them, and re-layouts  116 us (22%)
  matrix products  88.1 us (16%)
  loops' own time  55.3 us (10%)
  other arithmetic  52 us (10%)
  starting transfers between devices  18.3 us (3%)
  between operations  15.7 us (3%)
  blocking collectives  12.5 us (2%)
    psum x1, waiting for transfers between devices, shards(): combined = lax.psum(partial_mix, 'mp') + residual.astype(jnp.float32)  68.1 us
    another operation x1, loops' own time, shards(): heads_out = lax.map(one_head, jnp.arange(local_heads))  55.3 us
    reduce_scatter x1, waiting for transfers between devices, shards(): lax.psum_scatter(lax.dot_general(upstream_half, output_weight, (((1,), (1...  34.5 us
    dot_general x12, matrix products, one_head(): lax.dot_general(flat_query, cache_pair[0], (((1,), (1,)), ((), ())), pref...  30.3 us
    all_to_all x1, waiting for transfers between devices, shards(): lax.all_to_all(key_buffer, 'dp', split_axis=0, concat_axis=0, tiled=True)  25.4 us
    all_gather x1, waiting for transfers between devices, shards(): pooled_all = lax.all_gather(pooled_local, 'dp', axis=0, tiled=True)  23.6 us
    dot_general x12, matrix products, one_head(): jnp.dot(far_weight.astype(jnp.bfloat16), cache_pair[1], preferred_element...  22.2 us
    reduce_sum x12, other arithmetic, one_head(): jnp.sum(far_weight, axis=1).reshape(blocks, slot_count)  21.4 us
  transfers between devices with their start and end apart: 7, of which 6 were waited for; matrix products, arithmetic and copies ran while one was open for 8% of the time, Pallas kernels for 0%

commit v1 on v0

--- a/solution.py
+++ b/solution.py
@@ -142,7 +142,7 @@
     pooled_all = lax.all_gather(pooled_local, "dp", axis=0, tiled=True)
     partial_mix = jnp.dot(pooled_all, output_weight, preferred_element_type=jnp.float32)
     scaled_head = norm_gain * reward_head
-    combined = lax.psum(partial_mix, "mp") + residual.astype(jnp.float32)
+    combined = jnp.sum(lax.all_gather(partial_mix, "mp"), axis=0) + residual.astype(jnp.float32)
     square_sum = jnp.sum(combined * combined, axis=1)
     signal = jnp.sum(combined * scaled_head[None, :], axis=1)
     square_sum, signal = lax.psum((square_sum, signal), "dp")

time: 534 us -> 584 us (1.094)
  waiting for transfers between devices: 171 us -> 215 us
    all_gather x0 -> x1, waiting for transfers between devices: none -> 114 us  [shards(): lax.all_gather(partial_mix, 'mp')]
    psum x1 -> x0, waiting for transfers between devices: 68.1 us -> none  [shards(): combined = lax.psum(partial_mix, 'mp') + residual.astype(jnp.float32)]
  transfers between devices with their start and end apart: 7 -> 7, of which waited for: 6 -> 6; matrix products, arithmetic and copies ran while one was open for 8% -> 7% of each run, Pallas kernels for 0% -> 0%
where the time goes in v1:
time: 584 us; the launch traced here: 580 us
  waiting for transfers between devices  215 us (37%)
  local copies, waits for them, and re-layouts  116 us (20%)
  matrix products  88.3 us (15%)
  other arithmetic  56.8 us (10%)
  loops' own time  55.3 us (9%)
  starting transfers between devices  18.3 us (3%)
  between operations  15.7 us (3%)
  blocking collectives  13.8 us (2%)
    all_gather x1, waiting for transfers between devices, shards(): lax.all_gather(partial_mix, 'mp')  114 us
    another operation x1, loops' own time, shards(): heads_out = lax.map(one_head, jnp.arange(local_heads))  55.3 us
    reduce_scatter x1, waiting for transfers between devices, shards(): lax.psum_scatter(lax.dot_general(upstream_half, output_weight, (((1,), (1...  32.1 us
    dot_general x12, matrix products, one_head(): lax.dot_general(flat_query, cache_pair[0], (((1,), (1,)), ((), ())), pref...  30.3 us
    all_to_all x1, waiting for transfers between devices, shards(): lax.all_to_all(key_buffer, 'dp', split_axis=0, concat_axis=0, tiled=True)  25.4 us
    all_gather x1, waiting for transfers between devices, shards(): pooled_all = lax.all_gather(pooled_local, 'dp', axis=0, tiled=True)  23.6 us
    dot_general x12, matrix products, one_head(): jnp.dot(far_weight.astype(jnp.bfloat16), cache_pair[1], preferred_element...  22.2 us
    reduce_sum x12, other arithmetic, one_head(): jnp.sum(far_weight, axis=1).reshape(blocks, slot_count)  21.4 us
  transfers between devices with their start and end apart: 7, of which 6 were waited for; matrix products, arithmetic and copies ran while one was open for 7% of the time, Pallas kernels for 0%

profile of v1, /device:TPU:0, one launch (start us, length us, event | category | flops | bytes accessed | tf_op | source)
XLA Modules:
  0.0 579.8 jit_solution(12845692437926013171)
XLA Ops:
  10.4 5.2 all-to-all-start
  18.1 3.6 gather_fusion
  21.8 3.4 select_bitcast_fusion
  26.2 7.2 %scatter_fusion = bf16[48,8,1536]{2,1,0:T(8,128)(2,1)} fusion(bf16[48,8,1536]{2,1,0:T(8,128)(2,1)} %broadcast_in_dim.88, s32[48]{0:T(128)S(1)} %compare_select_fusion.6, bf16[48,8,1536]{2,1,0:T(8,128)(2,1)} %param.12), kind=kCustom, calls=%fused_computation.6 | custom fusion | bytes 3539136 | tf_op jit(solution)/shard_map/scatter | solution.py:65
  33.4 4.2 all-to-all-start.1
  43.2 8.2 %scatter_fusion.1 = bf16[48,8,3072]{2,1,0:T(8,128)(2,1)} fusion(bf16[48,8,3072]{2,1,0:T(8,128)(2,1)} %broadcast_in_dim.89, s32[48]{0:T(128)S(1)} %compare_select_fusion.6, bf16[48,8,3072]{2,1,0:T(8,128)(2,1)} %pad_maximum_fusion), kind=kCustom, calls=%fused_computation.7 | custom fusion | bytes 7078080 | tf_op jit(solution)/shard_map/scatter | solution.py:71
  51.4 3.1 all-to-all-done.1
  54.5 4.4 all-to-all-start.2
  58.9 2.7 dynamic-slice_bitcast_fusion.4
  62.9 25.4 %all-to-all-done.2 = bf16[8,6,8,3072]{3,2,1,0:T(8,128)(2,1)} async-done(((bf16[8,6,8,3072]{3,2,1,0:T(8,128)(2,1)}), bf16[8,6,8,3072]{3,2,1,0:T(8,128)(2,1)}, u32[]{:S(2)}, u32[]{:S(2)}) %all-to-all-start.2) | async-done | bytes 2359328 | tf_op jit(solution)/shard_map/all_to_all | solution.py:79
  88.9 239.0 %while.13 = (s32[]{:T(128)}, bf16[12,48,8,128]{3,2,0,1:T(8,128)(2,1)}, s32[12]{0:T(128)}, bf16[48,8,12,128]{3,1,2,0:T(8,128)(2,1)}, s32[12]{0:T(128)}, /*index=5...) while((s32[]{:T(128)}, ...), condition=%wide.region_9.10_spmd.clone.clone, body=%wide.region_4.9_spmd.clone.clone.sunk | while | flops 205486080 | bytes 6827307 | solution.py:135
  94.0 2.5 fusion.67
  113.9 2.5 fusion.67
  133.8 2.5 fusion.67
  153.7 2.5 fusion.67
  173.7 2.5 fusion.67
  213.5 2.5 fusion.67
  253.3 2.5 fusion.67
  293.2 2.5 fusion.67
  327.9 4.4 all-to-all-start.3
  332.4 16.7 %all-to-all-done.3 = bf16[8,6,8,1536]{3,2,1,0:T(8,128)(2,1)} async-done(((bf16[8,6,8,1536]{3,2,1,0:T(8,128)(2,1)}), bf16[8,6,8,1536]{3,2,1,0:T(8,128)(2,1)}, u32[]{:S(2)}, u32[]{:S(2)}) %all-to-all-start.3) | async-done | bytes 1179680 | tf_op jit(solution)/shard_map/all_to_all | solution.py:139
  349.2 3.0 gather_fusion.1
  352.1 3.2 gather_fusion.2
  355.4 23.6 %all-gather.4.cloned.1.call-done = bf16[384,1536]{1,0:T(8,128)(2,1)} async-done(((bf16[48,1536]{1,0:T(8,128)(2,1)}), bf16[384,1536]{1,0:T(8,128)(2,1)}) %all-gather.4.cloned.1.call-update) | async-done | bytes 1179664 | tf_op jit(solution)/shard_map/all_gather | solution.py:142
  378.9 3.8 fusion.44
  383.9 114.3 %all-gather.6.cloned.1.call-done = f32[1536,1024]{1,0:T(8,128)} async-done(((f32[384,1024]{1,0:T(8,128)}), f32[1536,1024]{1,0:T(8,128)}) %all-gather.6.cloned.1.call-update) | async-done | bytes 6291472 | tf_op jit(solution)/shard_map/all_gather | solution.py:145
  498.3 4.8 reduce_sum.75
  505.0 13.8 %all-reduce = (f32[384]{0:T(512)S(1)}, f32[384]{0:T(512)S(1)}) all-reduce(f32[384]{0:T(512)S(1)} %get-tuple-element.190, f32[384]{0:T(512)S(1)} %get-tuple-element.189), channel_id=1, replica_groups=mesh['dp'=8,'mp'=4] {'dp'}, use_global_device_ids=true, to_apply=%region_14.15 | all-reduce | flops 768 | bytes 6144 | tf_op jit(solution)/shard_map/psum | solution.py:148
  526.7 2.7 multiply_reduce_fusion
  530.3 2.9 fusion.46
  533.8 6.2 %fusion.45 = f32[1536,1024]{1,0:T(8,128)} fusion(bf16[384,1536]{1,0:T(8,128)(2,1)} %all-gather.4.cloned.1.call-done, bf16[384,1024]{1,0:T(8,128)(2,1)} %copy-done.3), kind=kOutput, calls=%fused_computation.102 | convolution fusion | flops 1207959552 | bytes 8257536 | tf_op jit(solution)/shard_map/dot_general | solution.py:157
  540.0 32.1 %reduce-scatter.2.cloned.1.call-done = f32[48,1536]{1,0:T(8,128)} async-done(((f32[384,1536]{1,0:T(8,128)}), f32[48,1536]{1,0:T(8,128)}) %reduce-scatter.2.cloned.1.call-update) | async-done | bytes 294928 | tf_op jit(solution)/shard_map/reduce_scatter | solution.py:160
  (366 shorter events, 189.5 us)
Async XLA Ops:
  7.2 371.8 %copy-start = (bf16[1536,1024]{1,0:T(8,128)(2,1)S(1)}, bf16[1536,1024]{1,0:T(8,128)(2,1)}, u32[]{:S(2)}) copy-start(bf16[1536,1024]{1,0:T(8,128)(2,1)} %param.19) | copy-start | bytes 9437188
  8.9 34.3 %copy-start.5 = (s32[48]{0:T(128)}, s32[48]{0:T(128)S(1)}, u32[]{:S(2)}) copy-start(s32[48]{0:T(128)S(1)} %compare_select_fusion.6) | copy-start | bytes 580
  10.4 23.0 %all-to-all-start = ((s32[8,1,6]{2,1,0:T(1,128)}), s32[8,1,6]{2,1,0:T(1,128)S(1)}, u32[]{:S(2)}, u32[]{:S(2)}) async-start(s32[8,1,6]{2,1,0:T(1,128)} %bitcast.10), calls=%async_computation | async-start | bytes 8192 | tf_op jit(solution)/shard_map/all_to_all | solution.py:80
  33.4 21.1 %all-to-all-start.1 = ((bf16[8,6,8,1536]{3,2,1,0:T(8,128)(2,1)}), bf16[8,6,8,1536]{3,2,1,0:T(8,128)(2,1)}, u32[]{:S(2)}, u32[]{:S(2)}) async-start(bf16[8,6,8,1536]{3,2,1,0:T(8,128)(2,1)} %bitcast.102), calls=%async_computation.1 | async-start | bytes 2359296 | tf_op jit(solution)/shard_map/all_to_all | solution.py:78
  54.5 33.8 %all-to-all-start.2 = ((bf16[8,6,8,3072]{3,2,1,0:T(8,128)(2,1)}), bf16[8,6,8,3072]{3,2,1,0:T(8,128)(2,1)}, u32[]{:S(2)}, u32[]{:S(2)}) async-start(bf16[8,6,8,3072]{3,2,1,0:T(8,128)(2,1)} %bitcast.101), calls=%async_computation.2 | async-start | bytes 4718592 | tf_op jit(solution)/shard_map/all_to_all | solution.py:79
  102.5 3.2 copy-start.2
  122.4 3.2 copy-start.2
  142.3 3.2 copy-start.2
  162.2 3.2 copy-start.2
  182.2 3.2 copy-start.2
  202.1 3.2 copy-start.2
  222.0 3.2 copy-start.2
  241.9 3.2 copy-start.2
  261.8 3.2 copy-start.2
  281.8 3.2 copy-start.2
  301.7 3.2 copy-start.2
  321.6 3.2 copy-start.2
  327.9 4.4 copy-start.6
  327.9 4.5 copy-start.9
  327.9 21.2 %all-to-all-start.3 = ((bf16[8,6,8,1536]{3,2,1,0:T(8,128)(2,1)}), bf16[8,6,8,1536]{3,2,1,0:T(8,128)(2,1)}, u32[]{:S(2)}, u32[]{:S(2)}) async-start(bf16[8,6,8,1536]{3,2,1,0:T(8,128)(2,1)} %bitcast.12), calls=%async_computation.3 | async-start | bytes 2359296 | tf_op jit(solution)/shard_map/all_to_all | solution.py:139
  332.3 46.6 %all-gather.4.cloned.1.call-start = ((), (), s32[]{:S(2)}) async-start(), calls=%async_computation.5 | async-start | bytes 1327104 | tf_op jit(solution)/shard_map/all_gather | solution.py:142
  355.3 143.0 %all-gather.6.cloned.1.call-start = ((), (), s32[]{:S(2)}) async-start(), calls=%async_computation.7 | async-start | bytes 7864320 | tf_op jit(solution)/shard_map/all_gather | solution.py:145
  382.7 0.7 copy-start.8
  382.7 1.1 copy-start.4
  382.7 1.1 copy-start.7
  382.8 189.4 %reduce-scatter.2.cloned.1.call-start = ((), (), s32[]{:S(2)}) async-start(), calls=%async_computation.6 | async-start | bytes 2654208 | tf_op jit(solution)/shard_map/reduce_scatter | solution.py:160
  518.9 7.8 %copy-start.1 = (f32[384]{0:T(512)}, f32[384]{0:T(512)S(1)}, u32[]{:S(2)}) copy-start(f32[384]{0:T(512)S(1)} %fusion.33) | copy-start | bytes 4612
  529.4 0.9 copy-start.3
Sparse Core Ops, SparseCore 0:
  355.4 23.4 all-gather.3
  382.9 115.3 all-gather.5
  533.3 38.8 reduce-scatter.1
